TPU v7x, 256 devices: a whole 4x4x8 slice. The times are simulated.
256 devices in a mesh: segment: 32 (over y_hi, z, core), tp: 8 (over x, y_lo).
Axes of the slice: x: 4, y: 4 (y_hi: 2, y_lo: 2; y = y_hi * 2 + y_lo), z: 8, core: 2. Of those that a mesh axis runs over, the one named last changes fastest.
Arguments:
- node_rows: bfloat16 [14336, 4096], P(('segment', 'tp')), may hold values from -6 to 6
- out_grad: bfloat16 [14336, 4096], P(('segment', 'tp')), may hold values from -6 to 6
- up_blocks: bfloat16 [1792, 16, 128, 128], P(('segment', 'tp')), may hold values from -0.125 to 0.125
- down_blocks: bfloat16 [1792, 16, 128, 128], P(('segment', 'tp')), may hold values from -0.0625 to 0.0625
- block_rows: int32 [1792, 16], P(('segment', 'tp')), may hold values from 0 to 31, as said below
Outputs:
- prev_grads: bfloat16 [14336, 4096], P(('segment', 'tp'))
Inputs may be any that keep to these rules, and one draw needn't show every extreme that they name: `block_rows`: each row names 16 distinct feature blocks in rising order.
All inputs are finite; a program needn't handle non-finite values.
Results may differ from a plain program's by a relative error of at most 0.015.
Values may be sent and summed in bfloat16 or wider, within the bound.
A program may use at most 192 MiB of HBM per device.

v0:
```python
import jax
import jax.numpy as jnp
from jax import lax
from jax.sharding import PartitionSpec as P

EPSILON = 1e-05


def partner_2(block, axis, stride):
    count = lax.axis_size(axis)
    route = []
    for low in range(count):
        high = low | 1 << stride
        if high != low and high < count:
            route += [(low, high), (high, low)]
    return lax.ppermute(block, axis, route)


def shifted(value, axis, steps):
    count = lax.axis_size(axis)
    pairs = [(source, (source + steps) % count) for source in range(count)]
    return lax.ppermute(value, axis, pairs)


def row_scale(rows):
    values = rows.astype(jnp.float32)
    inv_rms = lax.rsqrt(jnp.mean(values * values, axis=-1, keepdims=True) + EPSILON)
    return (values, inv_rms)


def column_sums(stacked_rows, up_blocks, down_blocks, block_rows):
    row_count = stacked_rows.shape[1]
    features = stacked_rows.shape[2]
    column_count, kept_count, block_size, _ = up_blocks.shape
    block_count = features // block_size
    values, inv_rms = row_scale(stacked_rows[0])
    normed = (values * inv_rms).astype(jnp.bfloat16)
    normed_blocks = normed.reshape(row_count, block_count, block_size)
    grad_blocks = stacked_rows[1].reshape(row_count, block_count, block_size)

    def column_step(total_grad, column):
        up_col, down_col, rows_col = column
        preact = jnp.einsum(
            "rkb,kbe->re", normed_blocks[:, rows_col], up_col, preferred_element_type=jnp.float32
        )
        hidden_grad = jnp.einsum(
            "rke,kfe->rf", grad_blocks[:, rows_col], down_col, preferred_element_type=jnp.float32
        )
        sigmoid_value = jax.nn.sigmoid(preact)
        slope_grad = (hidden_grad * sigmoid_value * (1.0 + preact * (1.0 - sigmoid_value))).astype(
            jnp.bfloat16
        )
        spread = jnp.einsum("rf,kbf->rkb", slope_grad, up_col, preferred_element_type=jnp.float32)
        return (total_grad.at[:, rows_col].add(spread), None)

    start_grad = jnp.zeros((row_count, block_count, block_size), jnp.float32)
    normal_grad, _ = lax.scan(column_step, start_grad, (up_blocks, down_blocks, block_rows))
    return normal_grad.reshape(row_count, features)


def body(node_rows, out_grad, up_blocks, down_blocks, block_rows):
    stacked = jnp.stack([node_rows, out_grad])
    gathered = lax.all_gather(stacked, "tp", axis=1, tiled=True)
    partner = partner_2(gathered, "segment", 0)
    gathered_all = jnp.concatenate([gathered, partner], axis=1)
    partial_grad = column_sums(gathered_all, up_blocks, down_blocks, block_rows)
    half_rows = gathered_all.shape[1] // 2
    received = partner_2(partial_grad[half_rows:].astype(jnp.bfloat16), "segment", 0).astype(
        jnp.float32
    )
    summed = lax.psum_scatter(
        (partial_grad[:half_rows] + received).astype(jnp.bfloat16),
        "tp",
        scatter_dimension=0,
        tiled=True,
    ).astype(jnp.float32)
    own_values, own_rms = row_scale(node_rows)
    mixed = jnp.mean(summed * own_values, axis=-1, keepdims=True)
    input_grad = (
        out_grad.astype(jnp.float32)
        + own_rms * summed
        - own_values * own_rms * own_rms * own_rms * mixed
    )
    input_grad = input_grad.astype(jnp.bfloat16)
    return shifted(input_grad, "segment", -2)


def solution(mesh):
    return jax.shard_map(
        body,
        mesh=mesh,
        in_specs=(
            P(("segment", "tp"), None),
            P(("segment", "tp"), None),
            P(("segment", "tp"), None, None, None),
            P(("segment", "tp"), None, None, None),
            P(("segment", "tp"), None),
        ),
        out_specs=P(("segment", "tp"), None),
        check_vma=False,
    )
```

profile of v0, /device:TPU:1, one launch (start us, length us, event | category | flops | bytes accessed | tf_op | source)
XLA Modules:
  0.0 683.4 jit_solution(14601369595243174533)
XLA Ops:
  9.7 155.1 %all-gather.2.cloned.1.call-done = bf16[2,448,4096]{2,0,1:T(2,128)(2,1)} async-done(((bf16[2,56,4096]{2,0,1:T(2,128)(2,1)}), bf16[2,448,4096]{2,0,1:T(2,128)(2,1)}) %all-gather.2.cloned.1.call-update) | async-done | bytes 7340048 | tf_op jit(solution)/shard_map/all_gather | solution.py:63
  164.9 11.4 %copy.18 = bf16[2,448,4096]{2,1,0:T(8,128)(2,1)} copy(bf16[2,448,4096]{2,0,1:T(2,128)(2,1)} %all-gather.2.cloned.1.call-done) | data formatting | bytes 14680064 | tf_op jit(solution)/shard_map/all_gather | solution.py:63
  177.0 21.0 %copy.19 = bf16[2,448,4096]{1,2,0:T(8,128)(2,1)} copy(bf16[2,448,4096]{2,0,1:T(2,128)(2,1)} %all-gather.2.cloned.1.call-done) | data formatting | bytes 14680064 | tf_op jit(solution)/shard_map/all_gather | solution.py:63
  197.9 11.6 %copy.20 = bf16[2,448,4096]{1,2,0:T(8,128)(2,1)} copy(bf16[2,448,4096]{2,1,0:T(8,128)(2,1)} %collective-permute-done) | data formatting | bytes 14680064 | tf_op jit(solution)/shard_map/ppermute | solution.py:16
  209.5 9.6 %fusion.46 = bf16[1,896,4096]{1,2,0:T(8,128)(2,1)} fusion(bf16[2,448,4096]{1,2,0:T(8,128)(2,1)} %copy.19, bf16[2,448,4096]{1,2,0:T(8,128)(2,1)} %copy.20), kind=kLoop, calls=%fused_computation.40 | loop fusion | flops 14680064 | bytes 22020096 | tf_op jit(solution)/shard_map/concatenate | solution.py:65
  220.5 6.8 %multiply_reduce_fusion = (f32[896]{0:T(1024)S(1)}, f32[1,896,4096]{1,2,0:T(8,128)}) fusion(bf16[2,448,4096]{1,2,0:T(8,128)(2,1)S(1)} %copy-done.1, bf16[2,448,4096]{1,2,0:T(8,128)(2,1)S(1)} %copy-done), kind=kLoop, calls=%fused_computation.39 | loop fusion | flops 22019200 | bytes 29363712 | tf_op jit(solution)/shard_map/reduce_sum | solution.py:27
  227.3 9.9 %multiply_convert_fusion = bf16[896,32,128]{0,2,1:T(8,128)(2,1)} fusion(f32[896,32,128]{0,2,1:T(8,128)} %bitcast.95, f32[896]{0:T(1024)S(1)} %add_rsqrt_fusion), kind=kLoop, calls=%fused_computation.38 | loop fusion | flops 7340032 | bytes 22023680 | tf_op jit(solution)/shard_map/convert_element_type | solution.py:37
  237.2 10.8 %copy.22 = bf16[896,32,128]{2,0,1:T(8,128)(2,1)} copy(bf16[896,32,128]{0,2,1:T(8,128)(2,1)} %multiply_convert_fusion) | data formatting | bytes 14680064 | tf_op jit(solution)/shard_map/while | solution.py:57
  248.0 10.7 %copy.21 = bf16[896,32,128]{2,0,1:T(8,128)(2,1)} copy(bf16[896,32,128]{0,2,1:T(8,128)(2,1)} %bitcast.96) | data formatting | bytes 14680064 | tf_op jit(solution)/shard_map/while | solution.py:57
  258.7 6.9 %broadcast_in_dim.2 = f32[896,32,128]{2,0,1:T(8,128)} broadcast(f32[]{:T(128)} %constant.6.clone.1), dimensions={} | broadcast | bytes 14680068 | tf_op jit(solution)/shard_map/broadcast_in_dim | solution.py:56
  265.6 292.2 %while.10 = (s32[]{:T(128)}, f32[896,32,128]{2,0,1:T(8,128)}, s32[7,16]{1,0:T(8,128)}, bf16[896,32,128]{2,0,1:T(8,128)(2,1)}, bf16[7,16,128,128]{3,2,1,0:T(8,128...) while((s32[]{:T(128)}, f32[896,32,128]{2,0,1:T(8,128)}, ...), condition=%wide.region_4.5_spmd, body=%wide.region_2.0_spmd.sunk | while | flops 1412154368 | bytes 53876196 | solution.py:57
  266.3 5.9 gather_fusion.1
  275.4 5.9 gather_fusion
  281.3 9.1 %convolution_bitcast_fusion.2 = f32[16,896,128]{2,1,0:T(8,128)} fusion(bf16[16,896,128]{2,1,0:T(8,128)(2,1)} %gather_fusion, bf16[7,16,128,128]{3,2,1,0:T(8,128)(2,1)} %get-tuple-element.140, s32[]{:T(128)S(6)} %copy.32, bf16[7,16,128,128]{3,2,1,0:T(8,128)(2,1)} %get-tuple-element.142, f32[896,128]{1,0:T(8,128)S(1)} %fusion.73), kind=kOutput, calls=%fused_computation.7.clone.1 | convolution fusion | flops 940556288 | bytes 12518400 | tf_op jit(solution)/shard_map/while/body/eval_jaxpr/rf,kbf->rkb/dot_general | solution.py:53
  290.4 16.9 %scatter_fusion = f32[896,32,128]{2,0,1:T(8,128)} fusion(f32[896,32,128]{2,0,1:T(8,128)} %get-tuple-element.129, s32[16]{0:T(128)S(1)} %fusion.72, f32[16,896,128]{2,1,0:T(8,128)} %convolution_bitcast_fusion.2), kind=kCustom, calls=%fused_computation.2.clone.1 | custom fusion | flops 1835008 | bytes 22020160 | tf_op jit(solution)/shard_map/while/body/eval_jaxpr/scatter-add | solution.py:54
  308.1 5.9 gather_fusion.1
  314.0 3.2 fusion.73
  317.2 5.9 gather_fusion
  323.1 9.1 %convolution_bitcast_fusion.2 = f32[16,896,128]{2,1,0:T(8,128)} fusion(bf16[16,896,128]{2,1,0:T(8,128)(2,1)} %gather_fusion, bf16[7,16,128,128]{3,2,1,0:T(8,128)(2,1)} %get-tuple-element.140, s32[]{:T(128)S(6)} %copy.32, bf16[7,16,128,128]{3,2,1,0:T(8,128)(2,1)} %get-tuple-element.142, f32[896,128]{1,0:T(8,128)S(1)} %fusion.73), kind=kOutput, calls=%fused_computation.7.clone.1 | convolution fusion | flops 940556288 | bytes 12518400 | tf_op jit(solution)/shard_map/while/body/eval_jaxpr/rf,kbf->rkb/dot_general | solution.py:53
  332.2 16.8 %scatter_fusion = f32[896,32,128]{2,0,1:T(8,128)} fusion(f32[896,32,128]{2,0,1:T(8,128)} %get-tuple-element.129, s32[16]{0:T(128)S(1)} %fusion.72, f32[16,896,128]{2,1,0:T(8,128)} %convolution_bitcast_fusion.2), kind=kCustom, calls=%fused_computation.2.clone.1 | custom fusion | flops 1835008 | bytes 22020160 | tf_op jit(solution)/shard_map/while/body/eval_jaxpr/scatter-add | solution.py:54
  349.8 5.9 gather_fusion.1
  355.7 3.3 fusion.73
  358.9 5.9 gather_fusion
  364.8 9.1 %convolution_bitcast_fusion.2 = f32[16,896,128]{2,1,0:T(8,128)} fusion(bf16[16,896,128]{2,1,0:T(8,128)(2,1)} %gather_fusion, bf16[7,16,128,128]{3,2,1,0:T(8,128)(2,1)} %get-tuple-element.140, s32[]{:T(128)S(6)} %copy.32, bf16[7,16,128,128]{3,2,1,0:T(8,128)(2,1)} %get-tuple-element.142, f32[896,128]{1,0:T(8,128)S(1)} %fusion.73), kind=kOutput, calls=%fused_computation.7.clone.1 | convolution fusion | flops 940556288 | bytes 12518400 | tf_op jit(solution)/shard_map/while/body/eval_jaxpr/rf,kbf->rkb/dot_general | solution.py:53
  373.9 16.9 %scatter_fusion = f32[896,32,128]{2,0,1:T(8,128)} fusion(f32[896,32,128]{2,0,1:T(8,128)} %get-tuple-element.129, s32[16]{0:T(128)S(1)} %fusion.72, f32[16,896,128]{2,1,0:T(8,128)} %convolution_bitcast_fusion.2), kind=kCustom, calls=%fused_computation.2.clone.1 | custom fusion | flops 1835008 | bytes 22020160 | tf_op jit(solution)/shard_map/while/body/eval_jaxpr/scatter-add | solution.py:54
  391.5 5.9 gather_fusion.1
  400.6 5.9 gather_fusion
  406.5 9.1 %convolution_bitcast_fusion.2 = f32[16,896,128]{2,1,0:T(8,128)} fusion(bf16[16,896,128]{2,1,0:T(8,128)(2,1)} %gather_fusion, bf16[7,16,128,128]{3,2,1,0:T(8,128)(2,1)} %get-tuple-element.140, s32[]{:T(128)S(6)} %copy.32, bf16[7,16,128,128]{3,2,1,0:T(8,128)(2,1)} %get-tuple-element.142, f32[896,128]{1,0:T(8,128)S(1)} %fusion.73), kind=kOutput, calls=%fused_computation.7.clone.1 | convolution fusion | flops 940556288 | bytes 12518400 | tf_op jit(solution)/shard_map/while/body/eval_jaxpr/rf,kbf->rkb/dot_general | solution.py:53
  415.6 16.9 %scatter_fusion = f32[896,32,128]{2,0,1:T(8,128)} fusion(f32[896,32,128]{2,0,1:T(8,128)} %get-tuple-element.129, s32[16]{0:T(128)S(1)} %fusion.72, f32[16,896,128]{2,1,0:T(8,128)} %convolution_bitcast_fusion.2), kind=kCustom, calls=%fused_computation.2.clone.1 | custom fusion | flops 1835008 | bytes 22020160 | tf_op jit(solution)/shard_map/while/body/eval_jaxpr/scatter-add | solution.py:54
  433.3 5.9 gather_fusion.1
  442.4 5.9 gather_fusion
  448.3 9.1 %convolution_bitcast_fusion.2 = f32[16,896,128]{2,1,0:T(8,128)} fusion(bf16[16,896,128]{2,1,0:T(8,128)(2,1)} %gather_fusion, bf16[7,16,128,128]{3,2,1,0:T(8,128)(2,1)} %get-tuple-element.140, s32[]{:T(128)S(6)} %copy.32, bf16[7,16,128,128]{3,2,1,0:T(8,128)(2,1)} %get-tuple-element.142, f32[896,128]{1,0:T(8,128)S(1)} %fusion.73), kind=kOutput, calls=%fused_computation.7.clone.1 | convolution fusion | flops 940556288 | bytes 12518400 | tf_op jit(solution)/shard_map/while/body/eval_jaxpr/rf,kbf->rkb/dot_general | solution.py:53
  457.4 16.9 %scatter_fusion = f32[896,32,128]{2,0,1:T(8,128)} fusion(f32[896,32,128]{2,0,1:T(8,128)} %get-tuple-element.129, s32[16]{0:T(128)S(1)} %fusion.72, f32[16,896,128]{2,1,0:T(8,128)} %convolution_bitcast_fusion.2), kind=kCustom, calls=%fused_computation.2.clone.1 | custom fusion | flops 1835008 | bytes 22020160 | tf_op jit(solution)/shard_map/while/body/eval_jaxpr/scatter-add | solution.py:54
  475.1 5.9 gather_fusion.1
  484.2 5.9 gather_fusion
  490.1 9.1 %convolution_bitcast_fusion.2 = f32[16,896,128]{2,1,0:T(8,128)} fusion(bf16[16,896,128]{2,1,0:T(8,128)(2,1)} %gather_fusion, bf16[7,16,128,128]{3,2,1,0:T(8,128)(2,1)} %get-tuple-element.140, s32[]{:T(128)S(6)} %copy.32, bf16[7,16,128,128]{3,2,1,0:T(8,128)(2,1)} %get-tuple-element.142, f32[896,128]{1,0:T(8,128)S(1)} %fusion.73), kind=kOutput, calls=%fused_computation.7.clone.1 | convolution fusion | flops 940556288 | bytes 12518400 | tf_op jit(solution)/shard_map/while/body/eval_jaxpr/rf,kbf->rkb/dot_general | solution.py:53
  499.2 16.9 %scatter_fusion = f32[896,32,128]{2,0,1:T(8,128)} fusion(f32[896,32,128]{2,0,1:T(8,128)} %get-tuple-element.129, s32[16]{0:T(128)S(1)} %fusion.72, f32[16,896,128]{2,1,0:T(8,128)} %convolution_bitcast_fusion.2), kind=kCustom, calls=%fused_computation.2.clone.1 | custom fusion | flops 1835008 | bytes 22020160 | tf_op jit(solution)/shard_map/while/body/eval_jaxpr/scatter-add | solution.py:54
  516.8 5.9 gather_fusion.1
  522.7 3.2 fusion.73
  526.0 5.9 gather_fusion
  531.9 9.1 %convolution_bitcast_fusion.2 = f32[16,896,128]{2,1,0:T(8,128)} fusion(bf16[16,896,128]{2,1,0:T(8,128)(2,1)} %gather_fusion, bf16[7,16,128,128]{3,2,1,0:T(8,128)(2,1)} %get-tuple-element.140, s32[]{:T(128)S(6)} %copy.32, bf16[7,16,128,128]{3,2,1,0:T(8,128)(2,1)} %get-tuple-element.142, f32[896,128]{1,0:T(8,128)S(1)} %fusion.73), kind=kOutput, calls=%fused_computation.7.clone.1 | convolution fusion | flops 940556288 | bytes 12518400 | tf_op jit(solution)/shard_map/while/body/eval_jaxpr/rf,kbf->rkb/dot_general | solution.py:53
  541.0 16.8 %scatter_fusion = f32[896,32,128]{2,0,1:T(8,128)} fusion(f32[896,32,128]{2,0,1:T(8,128)} %get-tuple-element.129, s32[16]{0:T(128)S(1)} %fusion.72, f32[16,896,128]{2,1,0:T(8,128)} %convolution_bitcast_fusion.2), kind=kCustom, calls=%fused_computation.2.clone.1 | custom fusion | flops 1835008 | bytes 22020160 | tf_op jit(solution)/shard_map/while/body/eval_jaxpr/scatter-add | solution.py:54
  557.8 3.6 copy_bitcast_fusion
  561.6 6.3 collective-permute-done.1
  567.9 6.0 fusion.47
  574.0 84.5 %reduce-scatter.2.cloned.1.call-done = bf16[56,4096]{1,0:T(8,128)(2,1)} async-done(((bf16[448,4096]{1,0:T(8,128)(2,1)}), bf16[56,4096]{1,0:T(8,128)(2,1)}) %reduce-scatter.2.cloned.1.call-update) | async-done | bytes 458768 | tf_op jit(solution)/shard_map/reduce_scatter | solution.py:71
  661.2 5.8 collective-permute-start.2
  666.9 8.9 %collective-permute-done.2 = bf16[56,4096]{1,0:T(8,128)(2,1)S(1)} collective-permute-done((bf16[56,4096]{1,0:T(8,128)(2,1)S(1)}, bf16[56,4096]{1,0:T(8,128)(2,1)S(1)}, u32[]{:S(2)}, u32[]{:S(2)}) %collective-permute-start.2) | collective-permute-done | bytes 458784 | tf_op jit(solution)/shard_map/ppermute | solution.py:22
  (40 shorter events, 26.8 us)
Async XLA Ops:
  6.5 158.3 %all-gather.2.cloned.1.call-start = ((), (), s32[]{:S(2)}) async-start(), calls=%async_computation.1 | async-start | bytes 8257536 | tf_op jit(solution)/shard_map/all_gather | solution.py:63
  9.7 648.8 %reduce-scatter.2.cloned.1.call-start = ((), (), s32[]{:S(2)}) async-start(), calls=%async_computation.2 | async-start | bytes 4128768 | tf_op jit(solution)/shard_map/reduce_scatter | solution.py:71
  176.3 21.7 %collective-permute-start = (bf16[2,448,4096]{2,1,0:T(8,128)(2,1)}, bf16[2,448,4096]{2,1,0:T(8,128)(2,1)}, u32[]{:S(2)}, u32[]{:S(2)}) collective-permute-start(bf16[2,448,4096]{2,1,0:T(8,128)(2,1)} %copy.18), channel_id=1, source_target_pairs={{0,8},{8,0},{16,24},{24,16},{32,40},{40,32},{48,56},{56,48},{64,72... | collective-permute-start | bytes 22020104 | tf_op jit(solution)/shard_map/ppermute | solution.py:16
  209.5 9.6 %copy-start = (bf16[2,448,4096]{1,2,0:T(8,128)(2,1)S(1)}, bf16[2,448,4096]{1,2,0:T(8,128)(2,1)}, u32[]{:S(2)}) copy-start(bf16[2,448,4096]{1,2,0:T(8,128)(2,1)} %copy.19) | copy-start | bytes 22020100
  209.5 10.9 %copy-start.1 = (bf16[2,448,4096]{1,2,0:T(8,128)(2,1)S(1)}, bf16[2,448,4096]{1,2,0:T(8,128)(2,1)}, u32[]{:S(2)}) copy-start(bf16[2,448,4096]{1,2,0:T(8,128)(2,1)} %copy.20) | copy-start | bytes 22020100
  561.4 97.0 %copy-start.2 = (bf16[56,4096]{1,0:T(8,128)(2,1)S(1)}, bf16[56,4096]{1,0:T(8,128)(2,1)}, u32[]{:S(2)}) copy-start(bf16[56,4096]{1,0:T(8,128)(2,1)} %param.7) | copy-start | bytes 1376260
  561.4 98.3 %copy-start.3 = (bf16[56,4096]{1,0:T(8,128)(2,1)S(1)}, bf16[56,4096]{1,0:T(8,128)(2,1)}, u32[]{:S(2)}) copy-start(bf16[56,4096]{1,0:T(8,128)(2,1)} %param.8) | copy-start | bytes 1376260
  561.4 6.5 collective-permute-start.1
  661.2 14.6 %collective-permute-start.2 = (bf16[56,4096]{1,0:T(8,128)(2,1)S(1)}, bf16[56,4096]{1,0:T(8,128)(2,1)S(1)}, u32[]{:S(2)}, u32[]{:S(2)}) collective-permute-start(bf16[56,4096]{1,0:T(8,128)(2,1)S(1)} %fusion.52), channel_id=1, source_target_pairs={{0,240},{8,248},{16,0},{24,8},{32,16},{40,24},{48,32},{56,40},{64,... | collective-permute-start | bytes 1376264 | tf_op jit(solution)/shard_map/ppermute | solution.py:22
Sparse Core Ops, SparseCore 0:
  9.8 155.0 all-gather.1
  574.1 84.3 reduce-scatter.1
where the time goes:
time: 687 us; the launch traced here: 683 us
  waiting for transfers between devices  255 us (37%)
  local copies, waits for them, and re-layouts  162 us (24%)
  other arithmetic  159 us (23%)
  matrix products  86.6 us (13%)
  between operations  13.5 us (2%)
    all_gather x1, waiting for transfers between devices, body(): gathered = lax.all_gather(stacked, 'tp', axis=1, tiled=True)  155 us
    scatter-add x7, other arithmetic, column_step(): return (total_grad.at[:, rows_col].add(spread), None)  118 us
    reduce_scatter x1, waiting for transfers between devices, body(): lax.psum_scatter((partial_grad[:half_rows] + received).astype(jnp.bfloat1...  84.5 us
    dot_general x7, matrix products, column_step(): jnp.einsum('rf,kbf->rkb', slope_grad, up_col, preferred_element_type=jnp....  63.8 us
    gather x7, local copies, waits for them, and re-layouts, column_step(): grad_blocks[:, rows_col]  41.3 us
    gather x7, local copies, waits for them, and re-layouts, column_step(): normed_blocks[:, rows_col]  41.2 us
    all_gather x2, local copies, waits for them, and re-layouts, body(): gathered = lax.all_gather(stacked, 'tp', axis=1, tiled=True)  32.4 us
    dot_general x7, matrix products, column_step(): jnp.einsum('rkb,kbe->re', normed_blocks[:, rows_col], up_col, preferred_e...  22.7 us
  transfers between devices with their start and end apart: 5, of which 4 were waited for; matrix products, arithmetic and copies ran while one was open for 3% of the time, Pallas kernels for 0%

commit v1 on v0

v1 whole, which is shorter than its diff:
```python
import functools

import jax
import jax.numpy as jnp
from jax import lax
from jax.experimental import pallas as pl
from jax.experimental.pallas import tpu as pltpu
from jax.sharding import PartitionSpec as P

EPSILON = 1e-05
MESH = pl.DeviceIdType.MESH
BF = jnp.bfloat16
F32 = jnp.float32
U = 128
HU = 16
PU = HU + 1
TP = 8

NAMES = (
    ["st", "nd", "iv", "A1", "A2", "A3a", "A3b", "B1", "B2", "C1a", "C1b", "C2a", "C2b", "C3", "C4"]
    + ["D1", "D2", "E1", "E2"]
    + [f"G{s}" for s in range(8)]
    + [f"M1_{s}" for s in range(8)]
    + ["M2_1", "M2_4", "M2_5", "M2_7", "pA", "pB6", "pB7", "mA", "mB6", "mB7"]
    + ["L0Am", "L0Ap", "L0Bp", "L0Bm", "L1Bp", "L1Bm", "R0Am", "R0Ap", "R0Bp", "R0Bm", "R1Bp", "R1Bm", "M6"]
)
SEM = {name: i for i, name in enumerate(NAMES)}
ZSEM = len(NAMES)


def cols(first, last):
    return pl.ds(first * U, (last - first) * U)


def kernel(
    rows, layers, inv_ref, node_ref, grad_ref, up_hbm, down_hbm, out_ref,
    x_ref, up_ref, down_ref, raw_up, raw_down, slope_ref, p_ref, sib_ref,
    ra_ref, rpa_ref, rpb_ref, rma_ref, rmb_ref, rl0_ref, rl1_ref, rr0_ref, rr1_ref, r6_ref,
    st_out, st_in, nd_out, nd_in, iv_out, iv_in, node_all, iv_all, fin_ref, land_ref,
    send_sem, recv_sem, local_sem,
):
    pair = 2 * rows
    hidden_blocks = raw_up.shape[0]
    features = up_ref.shape[0]
    half = features // 2
    seg, tp = lax.axis_index("segment"), lax.axis_index("tp")
    layer, core = seg // 2, seg % 2
    gx, gy = tp // 2, tp % 2

    def at_tp(x, y):
        return (seg, lax.rem(x + 4, 4) * 2 + y)

    sibling = (layer * 2 + 1 - core, tp)
    right, left = at_tp(gx + 1, gy), at_tp(gx - 1, gy)
    across = at_tp(gx, 1 - gy)
    before = lax.rem(layer + layers - 1, layers) * 2
    after = lax.rem(layer + 1, layers) * 2

    barrier = pltpu.get_barrier_semaphore()
    greet = [sibling, right, left, across]
    greet += [(before, tp), (before + 1, tp), (after, tp), (after + 1, tp)]
    for other in greet:
        pl.semaphore_signal(barrier, inc=1, device_id=other, device_id_type=MESH)

    raw = [
        pltpu.make_async_copy(up_hbm, raw_up.at[:, pl.ds(0, 16)], local_sem.at[0]),
        pltpu.make_async_copy(down_hbm, raw_down.at[:, pl.ds(0, 16)], local_sem.at[1]),
    ]
    for copy in raw:
        copy.start()

    def xs(slot, first=0, last=HU, side=0):
        return x_ref.at[:, side, slot // 2, pl.ds(pair * (slot % 2), pair), cols(first, last)]

    def ps(slot, first=0, last=PU, side=0):
        return p_ref.at[side, slot // 2, pl.ds(pair * (slot % 2), pair), cols(first, last)]

    table = {
        "st": (st_out, st_in, sibling),
        "nd": (nd_out, nd_in, sibling),
        "iv": (iv_out, iv_in, sibling),
        "A1": (xs(0), xs(3), right),
        "A2": (xs(0), xs(2), left),
        "A3a": (xs(0, 7, 16), xs(1, 7, 16), across),
        "A3b": (xs(0, 0, 7), xs(1, 0, 7), across),
        "B1": (xs(1, 7, 16), xs(5, 7, 16), right),
        "B2": (xs(1, 7, 16), xs(4, 7, 16), left),
        "C1a": (xs(3, 4, 7), xs(6, 4, 7), right),
        "C1b": (xs(3, 7, 12), xs(6, 7, 12), right),
        "C2a": (xs(2, 0, 4), xs(6, 0, 4), left),
        "C2b": (xs(2, 12, 16), xs(6, 12, 16), left),
        "C3": (xs(3, 0, 7), xs(5, 0, 7), across),
        "C4": (xs(2, 0, 7), xs(4, 0, 7), across),
        "D1": (xs(5, 7, 12), xs(7, 7, 12), right),
        "D2": (xs(4, 12, 16), xs(7, 12, 16), left),
        "E1": (xs(6, 4, 7), xs(7, 4, 7), across),
        "E2": (xs(6, 0, 4), xs(7, 0, 4), across),
        "M2_1": (ps(1, 0, 8), ra_ref.at[0], across),
        "M2_4": (ps(4, 0, 8), ra_ref.at[1], across),
        "M2_5": (ps(5, 0, 8), ra_ref.at[2], across),
        "M2_7": (ps(7, 0, 8), ra_ref.at[3], across),
        "pA": (ps(6, 4, 8), rpa_ref, right),
        "pB6": (ps(6, 8, 13), rpb_ref.at[0], right),
        "pB7": (ps(7, 8, 13), rpb_ref.at[1], right),
        "mA": (ps(6, 0, 4), rma_ref, left),
        "mB6": (ps(6, 13, 17), rmb_ref.at[0], left),
        "mB7": (ps(7, 13, 17), rmb_ref.at[1], left),
        "L0Am": (ps(2, 0, 4), rl0_ref.at[:, cols(0, 4)], right),
        "L0Ap": (ps(2, 4, 8), rl0_ref.at[:, cols(4, 8)], right),
        "L0Bp": (ps(2, 8, 13), rl0_ref.at[:, cols(8, 13)], right),
        "L0Bm": (ps(2, 13, 17), rl0_ref.at[:, cols(13, 17)], right),
        "L1Bp": (ps(4, 8, 13), rl1_ref.at[:, cols(0, 5)], right),
        "L1Bm": (ps(4, 13, 17), rl1_ref.at[:, cols(5, 9)], right),
        "R0Am": (ps(3, 0, 4), rr0_ref.at[:, cols(0, 4)], left),
        "R0Ap": (ps(3, 4, 8), rr0_ref.at[:, cols(4, 8)], left),
        "R0Bp": (ps(3, 8, 13), rr0_ref.at[:, cols(8, 13)], left),
        "R0Bm": (ps(3, 13, 17), rr0_ref.at[:, cols(13, 17)], left),
        "R1Bp": (ps(5, 8, 13), rr1_ref.at[:, cols(0, 5)], left),
        "R1Bm": (ps(5, 13, 17), rr1_ref.at[:, cols(5, 9)], left),
        "M6": (ps(1, 8, 17), r6_ref, across),
    }
    for s in range(8):
        table[f"G{s}"] = (xs(s), xs(s, side=1), sibling)
        table[f"M1_{s}"] = (ps(s, side=1), sib_ref.at[s], sibling)

    def remote(name):
        source, target, device = table[name]
        return pltpu.make_async_remote_copy(
            src_ref=source, dst_ref=target, send_sem=send_sem.at[SEM[name]],
            recv_sem=recv_sem.at[SEM[name]], device_id=device, device_id_type=MESH,
        )

    def start(*names):
        for name in names:
            remote(name).start()

    def arrived(*names):
        for name in names:
            remote(name).wait_recv()

    def grid_rows(body):
        lax.fori_loop(0, pair // 16, lambda i, _: (body(pl.ds(pl.multiple_of(i * 16, 16), 16)), 0)[1], 0)

    def add(slot, first, last, *others):
        base = pair * (slot % 2)

        def body(r):
            here = pl.ds(pl.multiple_of(r.start + base, 16), 16)
            total = p_ref[0, slot // 2, here, cols(first, last)].astype(F32)
            for ref, begin in others:
                total = total + ref[r, cols(begin, begin + last - first)].astype(F32)
            p_ref[0, slot // 2, here, cols(first, last)] = total.astype(BF)

        grid_rows(body)

    values = node_ref[...].astype(F32)
    inv_rms = lax.rsqrt(jnp.mean(values * values, axis=-1, keepdims=True) + EPSILON)
    mine = pl.ds(pl.multiple_of(core * half, half), half)
    theirs = pl.ds(pl.multiple_of((1 - core) * half, half), half)
    st_out[0, pl.ds(0, rows)] = (node_ref[:, theirs].astype(F32) * inv_rms).astype(BF)
    st_out[1, pl.ds(0, rows)] = grad_ref[:, theirs]
    pl.semaphore_wait(barrier, len(greet))
    start("st")
    nd_out[pl.ds(0, rows)] = node_ref[:, theirs]
    iv_out[...] = jnp.broadcast_to(inv_rms, iv_out.shape)
    start("nd", "iv")
    raw_up[:, 16] = jnp.zeros((hidden_blocks, U, U), BF)
    raw_down[:, 16] = jnp.zeros((hidden_blocks, U, U), BF)

    def both(own, other):
        own, other = own.astype(F32), other.astype(F32)
        first = core == 0
        return jnp.concatenate([jnp.where(first, own, other), jnp.where(first, other, own)], axis=0)

    arrived("st")
    own_normed = node_ref[:, mine].astype(F32) * inv_rms
    x_ref[0, 0, 0, pl.ds(0, pair)] = both(own_normed.astype(BF), st_in[0, pl.ds(0, rows)]).astype(BF)
    x_ref[1, 0, 0, pl.ds(0, pair)] = both(grad_ref[:, mine], st_in[1, pl.ds(0, rows)]).astype(BF)
    start("A1", "A2", "A3a", "A3b", "G0")
    arrived("nd", "iv")
    node_all[...] = both(node_ref[:, mine], nd_in[pl.ds(0, rows)]).astype(BF)
    iv_all[...] = both(iv_out[...], iv_in[...])

    for copy in raw:
        copy.wait()

    def densify(first, last):
        def body(i, _):
            c, f = i // 32, i % 32
            kept = inv_ref[c, lax.rem(f + core * 16, 32)]
            row = pl.ds(pl.multiple_of(f * U, U), U)
            col = pl.ds(pl.multiple_of(c * U, U), U)
            up_ref[row, col] = raw_up[c, kept]
            down_ref[row, col] = raw_down[c, kept].T
            return 0

        lax.fori_loop(first * 32, last * 32, body, 0)

    cut = (hidden_blocks + 1) // 2
    densify(0, cut)
    arrived("A3a")
    start("B1", "B2")
    densify(cut, hidden_blocks)
    arrived("A1", "A2", "A3b")
    start("C1a", "C2a", "C3", "C4", "C1b", "C2b", "G1", "G2", "G3")

    wide = min(512, half)

    def compute(g):
        def dot(a, b):
            return jnp.dot(a, b, preferred_element_type=F32)

        preact = dot(x_ref[0, 0, g], up_ref[pl.ds(0, half)]) + dot(x_ref[0, 1, g], up_ref[pl.ds(half, half)])
        hidden = dot(x_ref[1, 0, g], down_ref[pl.ds(0, half)]) + dot(x_ref[1, 1, g], down_ref[pl.ds(half, half)])
        s = jax.nn.sigmoid(preact)
        slope = (hidden * s * (1.0 + preact * (1.0 - s))).astype(BF)
        slope_ref[...] = slope
        row_sum = jnp.sum(slope.astype(F32) * preact, axis=-1, keepdims=True) * (1.0 / features)
        row_sum = jnp.broadcast_to(row_sum, (row_sum.shape[0], U)).astype(BF)
        p_ref[0, g, :, pl.ds(0, U)] = row_sum
        p_ref[1, g, :, pl.ds(0, U)] = row_sum
        steps = half // wide

        def body(j, _):
            w = up_ref[pl.ds(pl.multiple_of(j * wide, wide), wide), :]
            part = lax.dot_general(slope_ref[...], w, (((1,), (1,)), ((), ())), preferred_element_type=F32)
            at = pl.ds(pl.multiple_of(lax.rem(j, steps) * wide + U, U), wide)
            p_ref[j // steps, g, :, at] = part.astype(BF)
            return 0

        lax.fori_loop(0, 2 * steps, body, 0)

    def group(g, _):
        @pl.when(g == 0)
        def _():
            arrived("G0", "G1")

        @pl.when(g == 1)
        def _():
            arrived("B1", "B2")
            start("D1", "D2")
            arrived("G2", "G3")

        @pl.when(g == 2)
        def _():
            arrived("C1a", "C2a")
            start("E1", "E2")
            arrived("C3", "C4")
            start("G4", "G5")
            arrived("M1_0", "M1_1")
            add(0, 0, PU, (sib_ref.at[0], 0))
            add(1, 0, PU, (sib_ref.at[1], 0))
            arrived("C1b", "C2b")
            start("G6")
            arrived("G4", "G5")

        @pl.when(g == 3)
        def _():
            arrived("M1_2", "M1_3")
            add(2, 0, PU, (sib_ref.at[2], 0))
            add(3, 0, PU, (sib_ref.at[3], 0))
            start("M2_1", "L0Bm", "R0Bp")
            arrived("D1", "D2", "E1", "E2")
            start("G7")
            arrived("M1_4", "M1_5")
            add(4, 0, PU, (sib_ref.at[4], 0))
            add(5, 0, PU, (sib_ref.at[5], 0))
            start("M2_4", "M2_5", "L1Bm", "R1Bp")
            arrived("G6", "G7")

        compute(g)

        for k in range(4):
            @pl.when(g == k)
            def _(k=k):
                start(f"M1_{2 * k}", f"M1_{2 * k + 1}")

        return 0

    lax.fori_loop(0, 4, group, 0)

    arrived("M2_4", "M2_5")
    add(2, 0, 8, (ra_ref.at[1], 0))
    add(3, 0, 8, (ra_ref.at[2], 0))
    start("L0Am", "R0Ap")
    arrived("M1_7")
    add(7, 0, PU, (sib_ref.at[7], 0))
    start("M2_7", "pB7", "mB7")
    arrived("M1_6")
    add(6, 0, PU, (sib_ref.at[6], 0))
    start("pB6", "mB6")
    arrived("pB7")
    add(4, 8, 13, (rpb_ref.at[1], 0))
    start("L1Bp")
    arrived("mB7")
    add(5, 13, 17, (rmb_ref.at[1], 0))
    start("R1Bm")
    arrived("M2_7")
    add(6, 0, 8, (ra_ref.at[3], 0))
    start("pA", "mA")
    arrived("pB6")
    add(2, 8, 13, (rpb_ref.at[0], 0))
    start("L0Bp")
    arrived("mB6")
    add(3, 13, 17, (rmb_ref.at[0], 0))
    start("R0Bm")
    arrived("L1Bp", "L1Bm", "R1Bp", "R1Bm")
    add(1, 8, 17, (rl1_ref, 0), (rr1_ref, 0))
    start("M6")
    arrived("pA")
    add(2, 4, 8, (rpa_ref, 0))
    start("L0Ap")
    arrived("mA")
    add(3, 0, 4, (rma_ref, 0))
    start("R0Am")

    inv_all = iv_all[...]

    def finish(unit, *others):
        total = p_ref[0, 0, pl.ds(0, pair), cols(unit, unit + 1)].astype(F32)
        for ref, at in others:
            total = total + ref[:, cols(at, at + 1)].astype(F32)
        return total

    def emit(unit, total, scaled):
        at = cols(unit - 1, unit)
        result = x_ref[1, 0, 0, pl.ds(0, pair), at].astype(F32) + inv_all * total
        result = (result - node_all[:, at].astype(F32) * scaled)
        fin_ref[0, pl.ds(0, rows), at] = result[:rows].astype(BF)
        fin_ref[1, pl.ds(0, rows), at] = result[rows:].astype(BF)

    def shift(piece, first, last):
        copies = []
        for q in range(2):
            copies.append(pltpu.make_async_remote_copy(
                src_ref=fin_ref.at[q, :, cols(first, last)],
                dst_ref=land_ref.at[core, :, cols(first, last)],
                send_sem=send_sem.at[ZSEM + 2 * piece + q],
                recv_sem=recv_sem.at[ZSEM + 2 * piece + core],
                device_id=(before + q, tp), device_id_type=MESH,
            ))
        return copies

    def landed(piece, first, last, source):
        pltpu.make_async_remote_copy(
            src_ref=land_ref.at[source, :, cols(first, last)],
            dst_ref=land_ref.at[source, :, cols(first, last)],
            send_sem=send_sem.at[ZSEM + 2 * piece],
            recv_sem=recv_sem.at[ZSEM + 2 * piece + source],
            device_id=(before, tp), device_id_type=MESH,
        ).wait_recv()

    arrived("M2_1", "L0Am", "L0Ap", "R0Am", "R0Ap")
    scaled = inv_all * inv_all * finish(0, (ra_ref.at[0], 0), (rl0_ref, 0), (rr0_ref, 0))
    for unit in range(1, 8):
        emit(unit, finish(unit, (ra_ref.at[0], unit), (rl0_ref, unit), (rr0_ref, unit)), scaled)
    for copy in shift(0, 0, 7):
        copy.start()
    arrived("L0Bp", "L0Bm", "R0Bp", "R0Bm", "M6")
    for unit in range(8, 17):
        emit(unit, finish(unit, (rl0_ref, unit), (rr0_ref, unit), (r6_ref, unit - 8)), scaled)
    for copy in shift(1, 7, 16):
        copy.start()

    for piece, first, last in ((0, 0, 7), (1, 7, 16)):
        for source in range(2):
            landed(piece, first, last, source)
            at = pl.ds(source * half + first * U, (last - first) * U)
            out_ref[:, at] = land_ref[source, pl.ds(0, rows), cols(first, last)]
    for name in NAMES:
        remote(name).wait_send()
    for copy in shift(0, 0, 7) + shift(1, 7, 16):
        copy.wait_send()


def body(layers, node_rows, out_grad, up_blocks, down_blocks, block_rows):
    rows, features = node_rows.shape
    hidden_blocks, kept = block_rows.shape
    pair, half, hidden = 2 * rows, features // 2, hidden_blocks * U
    padded = (rows + 15) // 16 * 16
    wanted = block_rows[:, None, :] == jnp.arange(features // U, dtype=jnp.int32)[None, :, None]
    inverse = jnp.min(jnp.where(wanted, jnp.arange(kept, dtype=jnp.int32), kept), axis=-1)

    def vmem(*shape, dtype=BF):
        return pltpu.VMEM(shape, dtype)

    in_vmem = pl.BlockSpec(memory_space=pltpu.VMEM)
    return pl.pallas_call(
        functools.partial(kernel, rows, layers),
        out_shape=jax.ShapeDtypeStruct((rows, features), BF),
        in_specs=[
            pl.BlockSpec(memory_space=pltpu.SMEM), in_vmem, in_vmem,
            pl.BlockSpec(memory_space=pl.ANY), pl.BlockSpec(memory_space=pl.ANY),
        ],
        out_specs=in_vmem,
        scratch_shapes=[
            vmem(2, 2, 4, 2 * pair, half),
            vmem(features, hidden),
            vmem(features, hidden),
            vmem(hidden_blocks, kept + 1, U, U),
            vmem(hidden_blocks, kept + 1, U, U),
            vmem(2 * pair, hidden),
            vmem(2, 4, 2 * pair, PU * U),
            vmem(8, pair, PU * U),
            vmem(4, pair, 8 * U),
            vmem(pair, 4 * U),
            vmem(2, pair, 5 * U),
            vmem(pair, 4 * U),
            vmem(2, pair, 4 * U),
            vmem(pair, PU * U),
            vmem(pair, 9 * U),
            vmem(pair, PU * U),
            vmem(pair, 9 * U),
            vmem(pair, 9 * U),
            vmem(2, padded, half),
            vmem(2, padded, half),
            vmem(padded, half),
            vmem(padded, half),
            vmem(rows, U, dtype=F32),
            vmem(rows, U, dtype=F32),
            vmem(pair, half),
            vmem(pair, U, dtype=F32),
            vmem(2, padded, half),
            vmem(2, padded, half),
            pltpu.SemaphoreType.DMA((ZSEM + 4,)),
            pltpu.SemaphoreType.DMA((ZSEM + 4,)),
            pltpu.SemaphoreType.DMA((2,)),
        ],
        compiler_params=pltpu.CompilerParams(
            collective_id=0, has_side_effects=True, vmem_limit_bytes=60 * 2**20
        ),
        name="layer_grad",
    )(inverse, node_rows, out_grad, up_blocks, down_blocks)


def solution(mesh):
    layers = mesh.shape["segment"] // 2
    return jax.shard_map(
        functools.partial(body, layers),
        mesh=mesh,
        in_specs=(
            P(("segment", "tp"), None),
            P(("segment", "tp"), None),
            P(("segment", "tp"), None, None, None),
            P(("segment", "tp"), None, None, None),
            P(("segment", "tp"), None),
        ),
        out_specs=P(("segment", "tp"), None),
        check_vma=False,
    )
```

time: 687 us -> 122 us (0.18)
  waiting for transfers between devices: 255 us -> 0 us
  local copies, waits for them, and re-layouts: 162 us -> 1.82 us
  other arithmetic: 159 us -> 1.37 us
  Pallas kernels: 0 us -> 119 us
  matrix products: 86.6 us -> 0 us
  between operations: 13.5 us -> 0.01 us
    all_gather x1 -> x0, waiting for transfers between devices: 155 us -> none  [body(): gathered = lax.all_gather(stacked, 'tp', axis=1, tiled=True)]
    pallas_call x0 -> x1, Pallas kernels: none -> 119 us  [body(): pl.pallas_call(functools.partial(kernel, rows, layers), out_shape=jax.Sha...]
    scatter-add x7 -> x0, other arithmetic: 118 us -> none  [column_step(): return (total_grad.at[:, rows_col].add(spread), None)]
    dot_general x14 -> x0, matrix products: 86.6 us -> none  [the longest x7 63.8 us: column_step(): jnp.einsum('rf,kbf->rkb', slope_grad, up_col, preferred_element_type=jnp....]
    reduce_scatter x1 -> x0, waiting for transfers between devices: 84.5 us -> none  [body(): lax.psum_scatter((partial_grad[:half_rows] + received).astype(jnp.bfloat1...]
    gather x14 -> x0, local copies, waits for them, and re-layouts: 82.5 us -> none  [the longest x7 41.3 us: column_step(): grad_blocks[:, rows_col]]
    all_gather x2 -> x0, local copies, waits for them, and re-layouts: 32.4 us -> none  [body(): gathered = lax.all_gather(stacked, 'tp', axis=1, tiled=True)]
    while x2 -> x0, local copies, waits for them, and re-layouts: 21.4 us -> none  [column_sums(): lax.scan(column_step, start_grad, (up_blocks, down_blocks, block_rows))]
  transfers between devices with their start and end apart: 5 -> 0, of which waited for: 4 -> 0; matrix products, arithmetic and copies ran while one was open for 3% -> 0% of each run, Pallas kernels for 0% -> 0%
where the time goes in v1:
time: 122 us
  Pallas kernels  119 us (98%)
  local copies, waits for them, and re-layouts  1.82 us (1%)
  other arithmetic  1.37 us (1%)
    pallas_call x1, Pallas kernels, body(): pl.pallas_call(functools.partial(kernel, rows, layers), out_shape=jax.Sha...  119 us

profile of v1, /device:TPU:1, one launch (start us, length us, event | category | flops | bytes accessed | tf_op | source)
XLA Modules:
  0.0 121.8 jit_solution(16943407402298147403)
XLA Ops:
  0.0 1.4 %select_reduce_fusion.inv_ref = s32[7,32]{1,0:T(8,128)} fusion(s32[7,16]{1,0:T(8,128)} %param.9), kind=kLoop, calls=%fused_computation | loop fusion | flops 10528 | bytes 1344 | tf_op jit(solution)/shard_map/reduce_min | solution.py:382
  1.4 118.6 %layer_grad.1 = bf16[56,4096]{1,0:T(8,128)(2,1)} custom-call(s32[7,32]{1,0:T(8,128)} %select_reduce_fusion.inv_ref, bf16[56,4096]{1,0:T(8,128)(2,1)} %node_ref.1, bf16[56,4096]{1,0:T(8,128)(2,1)} %grad_ref.1, bf16[7,16,128,128]{3,2,1,0:T(8,128)(2,1)} %up_hbm.1, bf16[7,16,128,128]{3,2,1,0:T(8,128)(2,1)} %down_hbm.1), custom_call_target="tpu_custom_call" | custom-call | tf_op jit(solution)/shard_map/layer_grad/pallas_call | solution.py:388
  120.0 1.8 %copy.7 = bf16[56,4096]{1,0:T(8,128)(2,1)} copy(bf16[56,4096]{1,0:T(8,128)(2,1)} %layer_grad.1) | data formatting | bytes 917504

commit v2 on v0

v2 whole, which is shorter than its diff:
```python
import functools

import jax
import jax.numpy as jnp
from jax import lax
from jax.experimental import pallas as pl
from jax.experimental.pallas import tpu as pltpu
from jax.sharding import PartitionSpec as P

EPSILON = 1e-05
MESH = pl.DeviceIdType.MESH
BF = jnp.bfloat16
F32 = jnp.float32
U = 128
HU = 16
PU = HU + 1
TP = 8

PARTS = {
    "Ama": (0, 2), "Apa": (2, 4), "Amb": (4, 6), "Apb": (6, 8),
    "Bpa": (8, 11), "Bma": (11, 13), "Bpb": (13, 15), "Bmb": (15, 17),
}
AP, AM, BP, BM = ("Apa", "Apb"), ("Ama", "Amb"), ("Bpa", "Bpb"), ("Bma", "Bmb")


def named(head, *groups):
    return [head + part for group in groups for part in group]


NAMES = (
    ["sn", "sg", "nd", "iv", "A1", "A2", "A3a", "A3b", "B1f", "B1r", "B2f", "B2r", "C1a", "C1b", "C2a", "C2b", "C3", "C4"]
    + ["D1", "D2", "E1", "E2", "G7a", "G7b"]
    + [f"G{s}" for s in range(7)]
    + [f"M1_{s}" for s in range(8)]
    + ["M2_1", "M2_4", "M2_5", "M2_7", "M6a", "M6b"]
    + named("p6", AP, BP) + named("p7", BP) + named("m6", AM, BM) + named("m7", BM)
    + named("L0", AM, AP, BP, BM) + named("L1", BP, BM) + named("R0", AM, AP, BP, BM) + named("R1", BP, BM)
)
SEM = {name: i for i, name in enumerate(NAMES)}
ZSEM = len(NAMES)


def cols(first, last):
    return pl.ds(first * U, (last - first) * U)


def kernel(
    rows, layers, kept_ref, node_ref, grad_ref, up_hbm, down_hbm, out_ref,
    x_ref, up_ref, down_ref, raw_up, raw_down, slope_ref, p_ref, sib_ref,
    r6x_ref, r7x_ref, rl0_ref, rl1_ref, rr0_ref, rr1_ref, r6_ref,
    lent_ref, given_ref, iv_out, iv_in, node_all, iv_all, fin_ref, land_ref,
    send_sem, recv_sem, local_sem, ready_sem,
):
    pair = 2 * rows
    hidden_blocks = raw_up.shape[0]
    features = up_ref.shape[0]
    half = features // 2
    seg, tp = lax.axis_index("segment"), lax.axis_index("tp")
    layer, core = seg // 2, seg % 2
    gx, gy = tp // 2, tp % 2

    def at_tp(x, y):
        return (seg, lax.rem(x + 4, 4) * 2 + y)

    sibling = (layer * 2 + 1 - core, tp)
    right, left = at_tp(gx + 1, gy), at_tp(gx - 1, gy)
    across = at_tp(gx, 1 - gy)
    before = lax.rem(layer + layers - 1, layers) * 2
    after = lax.rem(layer + 1, layers) * 2

    barrier = pltpu.get_barrier_semaphore()
    greet = [sibling, right, left, across, (before, tp), (before + 1, tp)]
    for other in greet:
        pl.semaphore_signal(barrier, inc=1, device_id=other, device_id_type=MESH)

    load_up = pltpu.make_async_copy(up_hbm, raw_up.at[:, pl.ds(0, 16)], local_sem.at[0])
    load_down = pltpu.make_async_copy(down_hbm, raw_down.at[:, pl.ds(0, 16)], local_sem.at[1])
    load_up.start()
    load_down.start()

    def xs(slot, first=0, last=HU, side=0):
        return x_ref.at[:, side, pl.ds(pair * slot, pair), cols(first, last)]

    def ps(slot, first=0, last=PU, side=0):
        return p_ref.at[side, pl.ds(pair * slot, pair), cols(first, last)]

    padded = (rows + 15) // 16 * 16
    table = {
        "sn": (lent_ref.at[0], given_ref.at[0], sibling),
        "sg": (lent_ref.at[1], given_ref.at[1], sibling),
        "nd": (lent_ref.at[2], given_ref.at[2], sibling),
        "iv": (iv_out, iv_in, sibling),
        "A1": (xs(0), xs(3), right),
        "A2": (xs(0), xs(2), left),
        "A3a": (xs(0, 7, 16), xs(1, 7, 16), across),
        "A3b": (xs(0, 0, 7), xs(1, 0, 7), across),
        "B1f": (xs(1, 7, 12), xs(5, 7, 12), right),
        "B1r": (xs(1, 12, 16), xs(5, 12, 16), right),
        "B2f": (xs(1, 12, 16), xs(4, 12, 16), left),
        "B2r": (xs(1, 7, 12), xs(4, 7, 12), left),
        "C1a": (xs(3, 4, 7), xs(6, 4, 7), right),
        "C1b": (xs(3, 7, 12), xs(6, 7, 12), right),
        "C2a": (xs(2, 0, 4), xs(6, 0, 4), left),
        "C2b": (xs(2, 12, 16), xs(6, 12, 16), left),
        "C3": (xs(3, 0, 7), xs(5, 0, 7), across),
        "C4": (xs(2, 0, 7), xs(4, 0, 7), across),
        "D1": (xs(5, 7, 12), xs(7, 7, 12), right),
        "D2": (xs(4, 12, 16), xs(7, 12, 16), left),
        "E1": (xs(6, 4, 7), xs(7, 4, 7), across),
        "E2": (xs(6, 0, 4), xs(7, 0, 4), across),
        "M2_1": (ps(1, 0, 8), rl1_ref.at[:, cols(0, 8)], across),
        "M2_4": (ps(4, 0, 8), rr1_ref.at[:, cols(0, 8)], across),
        "M2_5": (ps(5, 0, 8), r7x_ref.at[:, cols(0, 8)], across),
        "M2_7": (ps(7, 0, 8), r6_ref.at[:, cols(0, 8)], across),
        "M6a": (ps(1, 8, 13), r6_ref.at[:, cols(8, 13)], across),
        "M6b": (ps(1, 13, 17), r6_ref.at[:, cols(13, 17)], across),
        "G7a": (xs(7, 0, 7), xs(7, 0, 7, side=1), sibling),
        "G7b": (xs(7, 7, 16), xs(7, 7, 16, side=1), sibling),
    }

    def along(head, slot, target, device, *groups):
        for part in [part for group in groups for part in group]:
            table[head + part] = (ps(slot, *PARTS[part]), target.at[:, cols(*PARTS[part])], device)

    along("p6", 6, r6x_ref, right, AP, BP)
    along("p7", 7, r7x_ref, right, BP)
    along("m6", 6, r6x_ref, left, AM, BM)
    along("m7", 7, r7x_ref, left, BM)
    along("L0", 2, rl0_ref, right, AM, AP, BP, BM)
    along("L1", 4, rl1_ref, right, BP, BM)
    along("R0", 3, rr0_ref, left, AM, AP, BP, BM)
    along("R1", 5, rr1_ref, left, BP, BM)
    for s in range(8):
        if s < 7:
            table[f"G{s}"] = (xs(s), xs(s, side=1), sibling)
        table[f"M1_{s}"] = (ps(s, side=1), sib_ref.at[s], sibling)

    def remote(name):
        source, target, device = table[name]
        return pltpu.make_async_remote_copy(
            src_ref=source, dst_ref=target, send_sem=send_sem.at[SEM[name]],
            recv_sem=recv_sem.at[SEM[name]], device_id=device, device_id_type=MESH,
        )

    def start(*names):
        for name in names:
            remote(name).start()

    def arrived(*names):
        for name in names:
            remote(name).wait_recv()

    def grid_rows(body):
        lax.fori_loop(0, pair // 16, lambda i, _: (body(pl.ds(pl.multiple_of(i * 16, 16), 16)), 0)[1], 0)

    def add(slot, first, last, *others):
        def body(r):
            here = pl.ds(pl.multiple_of(r.start + pair * slot, 16), 16)
            total = p_ref[0, here, cols(first, last)].astype(F32)
            for ref in others:
                total = total + ref[r, cols(first, last)].astype(F32)
            p_ref[0, here, cols(first, last)] = total.astype(BF)

        grid_rows(body)

    def add_sibling(*slots):
        for slot in slots:
            arrived(f"M1_{slot}")
            add(slot, 0, PU, sib_ref.at[slot])

    def pass_on(head, slot, landing, onward, *parts):
        for part in parts:
            arrived(head + part)
            add(slot, *PARTS[part], landing)
            start(onward + part)

    values = node_ref[...].astype(F32)
    inv_rms = lax.rsqrt(jnp.mean(values * values, axis=-1, keepdims=True) + EPSILON)
    mine = pl.ds(pl.multiple_of(core * half, half), half)
    theirs = pl.ds(pl.multiple_of((1 - core) * half, half), half)
    def lend(i, block):
        lent_ref[i] = jnp.concatenate(
            [block, jnp.zeros((padded - rows, half), F32)], axis=0
        ).astype(BF)

    lend(0, node_ref[:, theirs].astype(F32) * inv_rms)
    lend(1, grad_ref[:, theirs].astype(F32))
    pl.semaphore_wait(barrier, len(greet))
    for other in ((after, tp), (after + 1, tp)):
        pl.semaphore_signal(ready_sem, inc=1, device_id=other, device_id_type=MESH)
    start("sn", "sg")
    lend(2, node_ref[:, theirs].astype(F32))
    iv_out[...] = jnp.broadcast_to(inv_rms, iv_out.shape)
    start("nd", "iv")
    raw_up[:, 16] = jnp.zeros((hidden_blocks, U, U), BF)
    raw_down[:, 16] = jnp.zeros((hidden_blocks, U, U), BF)

    def given(i):
        return given_ref[i].astype(F32)[:rows]

    def both(own, other):
        own, other = own.astype(F32), other.astype(F32)
        first = core == 0
        return jnp.concatenate([jnp.where(first, own, other), jnp.where(first, other, own)], axis=0)

    arrived("sn", "sg")
    own_normed = node_ref[:, mine].astype(F32) * inv_rms
    x_ref[0, 0, pl.ds(0, pair)] = both(own_normed.astype(BF), given(0)).astype(BF)
    x_ref[1, 0, pl.ds(0, pair)] = both(grad_ref[:, mine], given(1)).astype(BF)
    start("A1", "A2", "A3a", "A3b", "G0")

    def densify(raw_ref, fill):
        def body(f, _):
            row = pl.ds(pl.multiple_of(f * U, U), U)
            fill(row, [raw_ref[c, kept_ref[c, lax.rem(f + core * 16, 32)]] for c in range(hidden_blocks)])
            return 0

        lax.fori_loop(0, 32, body, 0)

    def fill_up(row, blocks):
        up_ref[row, :] = jnp.concatenate(blocks, axis=1)

    def fill_down(row, blocks):
        down_ref[row, :] = jnp.concatenate(blocks, axis=0).T

    load_up.wait()
    load_down.wait()
    densify(raw_up, fill_up)
    arrived("nd", "iv")
    node_all[...] = both(node_ref[:, mine], given(2)).astype(BF)
    iv_all[...] = both(iv_out[...], iv_in[...])
    densify(raw_down, fill_down)

    wide = min(512, half)
    steps = half // wide

    def compute(begin, height, middle, later):
        r = pl.ds(begin, height)

        def dot(a, b):
            return jnp.dot(a, b, preferred_element_type=F32)

        preact = dot(x_ref[0, 0, r], up_ref[pl.ds(0, half)]) + dot(x_ref[0, 1, r], up_ref[pl.ds(half, half)])
        hidden = dot(x_ref[1, 0, r], down_ref[pl.ds(0, half)]) + dot(x_ref[1, 1, r], down_ref[pl.ds(half, half)])
        s = jax.nn.sigmoid(preact)
        slope = (hidden * s * (1.0 + preact * (1.0 - s))).astype(BF)
        slope_ref[pl.ds(0, height)] = slope
        row_sum = jnp.sum(slope.astype(F32) * preact, axis=-1, keepdims=True) * (1.0 / features)
        row_sum = jnp.broadcast_to(row_sum, (height, U)).astype(BF)
        p_ref[0, r, cols(8, 9)] = row_sum
        p_ref[1, r, cols(8, 9)] = row_sum
        middle()

        def spread(side):
            def body(j, _):
                w = up_ref[pl.ds(pl.multiple_of(side * half + j * wide, wide), wide), :]
                at = j * wide + j // (steps // 2) * U
                part = lax.dot_general(
                    slope_ref[pl.ds(0, height)], w, (((1,), (1,)), ((), ())), preferred_element_type=F32
                )
                p_ref[side, r, pl.ds(pl.multiple_of(at, U), wide)] = part.astype(BF)
                return 0

            lax.fori_loop(0, steps, body, 0)

        spread(1)
        spread(0)
        later()

    arrived("G0")
    compute(0, pair, lambda: None, lambda: start("M1_0"))
    arrived("A1", "A2", "A3a", "A3b")
    start("B1f", "B2f", "C1a", "C2a", "C3", "C4", "G1", "G2", "G3")
    add_sibling(0)
    arrived("G1", "G2", "G3")

    def mid_1():
        start("B1r", "B2r")
        arrived("C1a", "C2a")
        start("E1", "E2")

    compute(pair, 3 * pair, mid_1, lambda: start("M1_1", "M1_2", "M1_3"))
    arrived("B1f", "B2f")
    start("D1", "D2")
    arrived("C3", "B2r")
    arrived("C4", "B1r")
    start("G4", "G5", "C1b", "C2b")
    add_sibling(1, 2, 3)
    start("M2_1", *named("L0", BM), *named("R0", BP))
    arrived("G4", "G5")

    def mid_4():
        arrived("D1", "D2")
        start("G7b")

    def later_4():
        start("M1_4", "M1_5")
        arrived("E1", "E2")
        start("G7a")

    compute(4 * pair, 2 * pair, mid_4, later_4)

    def single(i):
        def before_7():
            add_sibling(4, 5)
            start("M2_4", "M2_5", *named("L1", BM), *named("R1", BP))
            arrived("G7a", "G7b")

        def before_6():
            add_sibling(7)
            start("M2_7", *named("p7", BP), *named("m7", BM))
            arrived("G6")

        def mid_7():
            arrived("C1b", "C2b")
            start("G6")

        def mid_6():
            arrived("M2_4")
            add(2, 0, 8, rr1_ref)
            start(*named("L0", AM))
            arrived("M2_5")
            add(3, 0, 8, r7x_ref)
            start(*named("R0", AP))
            pass_on("p7", 4, r7x_ref, "L1", *BP)
            pass_on("m7", 5, r7x_ref, "R1", *BM)

        def choose(first, second):
            (first, second)[i]()

        choose(before_7, before_6)
        compute(
            (7 - i) * pair, pair,
            lambda: choose(mid_7, mid_6),
            lambda: choose(lambda: start("M1_7"), lambda: start("M1_6")),
        )

    single(0)
    single(1)

    add_sibling(6)
    start("p6Bpa", "m6Bma", "p6Bpb", "m6Bmb")
    arrived("M2_7")
    add(6, 0, 8, r6_ref)
    start("p6Apa", "m6Ama", "p6Apb", "m6Amb")
    arrived("L1Bpa", "L1Bma", "R1Bpa", "R1Bma")
    add(1, 8, 13, rl1_ref, rr1_ref)
    start("M6a")
    pass_on("p6", 2, r6x_ref, "L0", "Bpa")
    pass_on("m6", 3, r6x_ref, "R0", "Bma")
    arrived("L1Bpb", "L1Bmb", "R1Bpb", "R1Bmb")
    add(1, 13, 17, rl1_ref, rr1_ref)
    start("M6b")
    pass_on("p6", 2, r6x_ref, "L0", "Bpb")
    pass_on("m6", 3, r6x_ref, "R0", "Bmb")
    pass_on("p6", 2, r6x_ref, "L0", "Apa")
    pass_on("m6", 3, r6x_ref, "R0", "Ama")
    pass_on("p6", 2, r6x_ref, "L0", "Apb")
    pass_on("m6", 3, r6x_ref, "R0", "Amb")

    inv_all = iv_all[...]

    def finish(unit, *others):
        total = p_ref[0, pl.ds(0, pair), cols(unit, unit + 1)].astype(F32)
        for ref in others:
            total = total + ref[:, cols(unit, unit + 1)].astype(F32)
        return total

    order = (8, 9, 10, 11, 12, 13, 14, 15, 0, 1, 2, 3, 4, 5, 6, 7)

    def emit(place, scaled):
        halves = []
        for unit in order[2 * place : 2 * place + 2]:
            landings = (rl1_ref, rl0_ref, rr0_ref) if unit < 8 else (rl0_ref, rr0_ref, r6_ref)
            at = cols(unit, unit + 1)
            result = x_ref[1, 0, pl.ds(0, pair), at].astype(F32) + inv_all * finish(unit + unit // 8, *landings)
            halves.append(result - node_all[:, at].astype(F32) * scaled)
        for q in range(2):
            both_units = [part[q * rows : (q + 1) * rows] for part in halves]
            fin_ref[q, place] = jnp.concatenate(both_units, axis=0).astype(BF)

    pieces = ((0, 2), (2, 4), (4, 6), (6, 8))

    def shift(piece):
        first, last = pieces[piece]
        copies = []
        for q in range(2):
            copies.append(pltpu.make_async_remote_copy(
                src_ref=fin_ref.at[q, pl.ds(first, last - first)],
                dst_ref=land_ref.at[core, pl.ds(first, last - first)],
                send_sem=send_sem.at[ZSEM + 2 * piece + q],
                recv_sem=recv_sem.at[ZSEM + 2 * piece + core],
                device_id=(before + q, tp), device_id_type=MESH,
            ))
        return copies

    def landed(piece, source):
        first, last = pieces[piece]
        there = land_ref.at[source, pl.ds(first, last - first)]
        pltpu.make_async_remote_copy(
            src_ref=there, dst_ref=there, send_sem=send_sem.at[ZSEM + 2 * piece],
            recv_sem=recv_sem.at[ZSEM + 2 * piece + source], device_id=(before, tp), device_id_type=MESH,
        ).wait_recv()

    def finished(piece, scaled):
        for place in range(*pieces[piece]):
            emit(place, scaled)
        for copy in shift(piece):
            copy.start()

    pl.semaphore_wait(ready_sem, 2)
    arrived("L0Bpa", "L0Bma", "R0Bpa", "R0Bma", "M6a")
    scaled = inv_all * inv_all * finish(8, rl0_ref, rr0_ref, r6_ref)
    finished(0, scaled)
    arrived("L0Bpb", "L0Bmb", "R0Bpb", "R0Bmb", "M6b")
    finished(1, scaled)
    arrived("M2_1", "L0Ama", "L0Apa", "R0Ama", "R0Apa")
    finished(2, scaled)
    arrived("L0Amb", "L0Apb", "R0Amb", "R0Apb")
    finished(3, scaled)

    for piece, (first, last) in enumerate(pieces):
        for source in range(2):
            landed(piece, source)
            for place in range(first, last):
                units = land_ref[source, place].astype(F32)
                for i, unit in enumerate(order[2 * place : 2 * place + 2]):
                    at = pl.ds(source * half + unit * U, U)
                    out_ref[:, at] = units[i * rows : (i + 1) * rows].astype(BF)
    for name in NAMES:
        remote(name).wait_send()
    for piece in range(len(pieces)):
        for copy in shift(piece):
            copy.wait_send()


def body(layers, node_rows, out_grad, up_blocks, down_blocks, block_rows):
    rows, features = node_rows.shape
    hidden_blocks, kept = block_rows.shape
    pair, half, hidden = 2 * rows, features // 2, hidden_blocks * U
    padded = (rows + 15) // 16 * 16
    wanted = block_rows[:, None, :] == jnp.arange(features // U, dtype=jnp.int32)[None, :, None]
    inverse = jnp.min(jnp.where(wanted, jnp.arange(kept, dtype=jnp.int32), kept), axis=-1)

    def vmem(*shape, dtype=BF):
        return pltpu.VMEM(shape, dtype)

    in_vmem = pl.BlockSpec(memory_space=pltpu.VMEM)
    return pl.pallas_call(
        functools.partial(kernel, rows, layers),
        out_shape=jax.ShapeDtypeStruct((rows, features), BF),
        in_specs=[
            pl.BlockSpec(memory_space=pltpu.SMEM), in_vmem, in_vmem,
            pl.BlockSpec(memory_space=pl.ANY), pl.BlockSpec(memory_space=pl.ANY),
        ],
        out_specs=in_vmem,
        scratch_shapes=[
            vmem(2, 2, TP * pair, half),
            vmem(features, hidden),
            vmem(features, hidden),
            vmem(hidden_blocks, kept + 1, U, U),
            vmem(hidden_blocks, kept + 1, U, U),
            vmem(3 * pair, hidden),
            vmem(2, TP * pair, PU * U),
            vmem(8, pair, PU * U),
            *[vmem(pair, PU * U) for _ in range(7)],
            vmem(3, padded, half),
            vmem(3, padded, half),
            vmem(rows, U, dtype=F32),
            vmem(rows, U, dtype=F32),
            vmem(pair, half),
            vmem(pair, U, dtype=F32),
            vmem(2, HU // 2, pair, U),
            vmem(2, HU // 2, pair, U),
            pltpu.SemaphoreType.DMA((ZSEM + 8,)),
            pltpu.SemaphoreType.DMA((ZSEM + 8,)),
            pltpu.SemaphoreType.DMA((2,)),
            pltpu.SemaphoreType.REGULAR,
        ],
        compiler_params=pltpu.CompilerParams(
            collective_id=0, has_side_effects=True, vmem_limit_bytes=62 * 2**20
        ),
        name="layer_grad",
    )(inverse, node_rows, out_grad, up_blocks, down_blocks)


def solution(mesh):
    layers = mesh.shape["segment"] // 2
    return jax.shard_map(
        functools.partial(body, layers),
        mesh=mesh,
        in_specs=(
            P(("segment", "tp"), None),
            P(("segment", "tp"), None),
            P(("segment", "tp"), None, None, None),
            P(("segment", "tp"), None, None, None),
            P(("segment", "tp"), None),
        ),
        out_specs=P(("segment", "tp"), None),
        check_vma=False,
    )
```

time: 687 us -> 110 us (0.16)
  waiting for transfers between devices: 255 us -> 0 us
  local copies, waits for them, and re-layouts: 162 us -> 1.82 us
  other arithmetic: 159 us -> 1.37 us
  Pallas kernels: 0 us -> 107 us
  matrix products: 86.6 us -> 0 us
  between operations: 13.5 us -> 0.01 us
    all_gather x1 -> x0, waiting for transfers between devices: 155 us -> none  [body(): gathered = lax.all_gather(stacked, 'tp', axis=1, tiled=True)]
    scatter-add x7 -> x0, other arithmetic: 118 us -> none  [column_step(): return (total_grad.at[:, rows_col].add(spread), None)]
    pallas_call x0 -> x1, Pallas kernels: none -> 107 us  [body(): pl.pallas_call(functools.partial(kernel, rows, layers), out_shape=jax.Sha...]
    dot_general x14 -> x0, matrix products: 86.6 us -> none  [the longest x7 63.8 us: column_step(): jnp.einsum('rf,kbf->rkb', slope_grad, up_col, preferred_element_type=jnp....]
    reduce_scatter x1 -> x0, waiting for transfers between devices: 84.5 us -> none  [body(): lax.psum_scatter((partial_grad[:half_rows] + received).astype(jnp.bfloat1...]
    gather x14 -> x0, local copies, waits for them, and re-layouts: 82.5 us -> none  [the longest x7 41.3 us: column_step(): grad_blocks[:, rows_col]]
    all_gather x2 -> x0, local copies, waits for them, and re-layouts: 32.4 us -> none  [body(): gathered = lax.all_gather(stacked, 'tp', axis=1, tiled=True)]
    while x2 -> x0, local copies, waits for them, and re-layouts: 21.4 us -> none  [column_sums(): lax.scan(column_step, start_grad, (up_blocks, down_blocks, block_rows))]
  transfers between devices with their start and end apart: 5 -> 0, of which waited for: 4 -> 0; matrix products, arithmetic and copies ran while one was open for 3% -> 0% of each run, Pallas kernels for 0% -> 0%
where the time goes in v2:
time: 110 us
  Pallas kernels  107 us (97%)
  local copies, waits for them, and re-layouts  1.82 us (2%)
  other arithmetic  1.37 us (1%)
    pallas_call x1, Pallas kernels, body(): pl.pallas_call(functools.partial(kernel, rows, layers), out_shape=jax.Sha...  107 us

profile of v2, /device:TPU:1, one launch (start us, length us, event | category | flops | bytes accessed | tf_op | source)
XLA Modules:
  0.0 109.8 jit_solution(15347885865286509413)
XLA Ops:
  0.0 1.4 %select_reduce_fusion.kept_ref = s32[7,32]{1,0:T(8,128)} fusion(s32[7,16]{1,0:T(8,128)} %param.9), kind=kLoop, calls=%fused_computation | loop fusion | flops 10528 | bytes 1344 | tf_op jit(solution)/shard_map/reduce_min | solution.py:443
  1.4 106.6 %layer_grad.1 = bf16[56,4096]{1,0:T(8,128)(2,1)} custom-call(s32[7,32]{1,0:T(8,128)} %select_reduce_fusion.kept_ref, bf16[56,4096]{1,0:T(8,128)(2,1)} %node_ref.1, bf16[56,4096]{1,0:T(8,128)(2,1)} %grad_ref.1, bf16[7,16,128,128]{3,2,1,0:T(8,128)(2,1)} %up_hbm.1, bf16[7,16,128,128]{3,2,1,0:T(8,128)(2,1)} %down_hbm.1), custom_call_target="tpu_custom_call" | custom-call | tf_op jit(solution)/shard_map/layer_grad/pallas_call | solution.py:449
  108.0 1.8 %copy.7 = bf16[56,4096]{1,0:T(8,128)(2,1)} copy(bf16[56,4096]{1,0:T(8,128)(2,1)} %layer_grad.1) | data formatting | bytes 917504
